TPU v7x, 256 devices: a whole 4x4x8 slice. The times are simulated.
256 devices in a mesh: gx: 8 (over z_hi, core), gy: 4 (over y), gz: 8 (over x, z_lo).
Axes of the slice: x: 4, y: 4, z: 8 (z_hi: 4, z_lo: 2; z = z_hi * 2 + z_lo), core: 2. Of those that a mesh axis runs over, the one named last changes fastest.
Arguments:
- latent: bfloat16 [64, 64, 128, 256], P('gx', 'gy', 'gz'), may hold values from -700 to 700
- norm_gain: float32 [256], replicated, may hold values from 0.5 to 1.5
- norm_shift: float32 [256], replicated, may hold values from -3 to 3
- w_qkv: bfloat16 [256, 768], replicated, may hold values from -40 to 40
- w_out: bfloat16 [256, 256], replicated, may hold values from -0.375 to 0.375
- b_out: float32 [256], replicated, may hold values from -3 to 3
- depth_limit: int32 [16, 16, 32], P('gx', 'gy', 'gz'), may hold values from 0 to 1
Outputs:
- attended_out: bfloat16 [64, 64, 128, 256], P('gx', 'gy', 'gz')
All inputs are finite; a program needn't handle non-finite values.
Results may differ from a plain program's by a relative error of at most 0.038.
Values may be sent and summed in bfloat16 or wider, within the bound.
No kernel may reach another device: no remote copies, remote signals or barrier semaphores. Data moves between devices by JAX's collectives and lax.ppermute only.
A program may use at most 128 MiB of HBM per device.

v0:
```python
import jax
import jax.numpy as jnp
import numpy as np
from jax import lax
from jax.sharding import PartitionSpec as P

HEADS = 8
GROUPS = 32


neighbour_offsets = [
    (first, second, third) for first in range(3) for second in range(3) for third in range(3)
]


def padded_2(cells, sides, width):
    for axis, dim in sides:
        count = lax.axis_size(axis)
        ends = count - 1
        head = lax.slice_in_dim(cells, 0, width, axis=dim)
        tail = lax.slice_in_dim(cells, cells.shape[dim] - width, cells.shape[dim], axis=dim)
        cells = jnp.concatenate(
            [
                lax.ppermute(tail, axis, [(i, (i + 1) % count) for i in range(ends)]),
                cells,
                lax.ppermute(head, axis, [((i + 1) % count, i) for i in range(ends)]),
            ],
            axis=dim,
        )
    return cells


def to_blocks(field):
    size_x, size_y, size_z, chans = field.shape
    shaped = field.reshape(size_x // 4, 4, size_y // 4, 4, size_z // 4, 4, chans)
    return shaped.transpose(0, 2, 4, 1, 3, 5, 6).reshape(
        size_x // 4, size_y // 4, size_z // 4, 64, chans
    )


def from_blocks(blocks):
    count_x, count_y, count_z, cells, chans = blocks.shape
    shaped = blocks.reshape(count_x, count_y, count_z, 4, 4, 4, chans)
    return shaped.transpose(0, 3, 1, 4, 2, 5, 6).reshape(
        count_x * 4, count_y * 4, count_z * 4, chans
    )


def valid_table(limit, start_x, start_y, start_z, total_x, total_y, total_z):
    table = jnp.asarray(np.array(neighbour_offsets, dtype=np.int32) - 1)
    index_x = start_x + jnp.arange(limit.shape[0], dtype=jnp.int32)
    index_y = start_y + jnp.arange(limit.shape[1], dtype=jnp.int32)
    index_z = start_z + jnp.arange(limit.shape[2], dtype=jnp.int32)
    key_x = index_x[:, None] + table[None, :, 0]
    key_y = index_y[:, None] + table[None, :, 1]
    key_z = index_z[:, None] + table[None, :, 2]
    inside_x = (key_x >= 0) & (key_x < total_x)
    inside_y = (key_y >= 0) & (key_y < total_y)
    inside_z = (key_z >= 0) & (key_z < total_z)
    depth_ok = jnp.abs(table[:, 2])[None, None, None, :] <= limit[..., None]
    return (
        inside_x[:, None, None, :]
        & inside_y[None, :, None, :]
        & inside_z[None, None, :, :]
        & depth_ok
    )


def attend_span(query_blocks, region, valid, heads):
    depth = query_blocks.shape[1]
    width = query_blocks.shape[-1]
    head_dim = width // heads
    pieces = [
        region[first, second : second + 2, third : third + depth]
        for first, second, third in neighbour_offsets
    ]
    keyvals = jnp.stack(pieces, axis=2).reshape(2, depth, 27 * 64, 2 * width)
    keys = keyvals[..., :width].reshape(2, depth, 27 * 64, heads, head_dim)
    values = keyvals[..., width:].reshape(2, depth, 27 * 64, heads, head_dim)
    queries = query_blocks.reshape(2, depth, 64, heads, head_dim)
    scores = jnp.einsum(
        "abqhd,abkhd->abhqk", queries, keys, preferred_element_type=jnp.float32
    ) * head_dim ** (-0.5)
    allowed = jnp.repeat(valid, 64, axis=-1)
    scores = jnp.where(allowed[:, :, None, None, :], scores, jnp.float32(-1e30))
    top = jnp.max(scores, axis=-1, keepdims=True)
    expd = jnp.exp(scores - top)
    weights = (expd / jnp.sum(expd, axis=-1, keepdims=True)).astype(jnp.bfloat16)
    mixed = jnp.einsum("abhqk,abkhd->abqhd", weights, values, preferred_element_type=jnp.float32)
    return mixed.astype(jnp.bfloat16).reshape(2, depth, 64, width)


def attend_all(query_blocks, kv_blocks, valid, heads):
    count_x, count_y, count_z = query_blocks.shape[:3]
    width = query_blocks.shape[-1]
    pairs = count_y // 2
    zero = jnp.zeros((), jnp.int32)

    def one_span(index):
        block_x = index // pairs
        block_y = index % pairs * 2
        query_part = lax.dynamic_slice(
            query_blocks, (block_x, block_y, zero, zero, zero), (1, 2, count_z, 64, width)
        )[0]
        region = lax.dynamic_slice(
            kv_blocks, (block_x, block_y, zero, zero, zero), (3, 4, count_z + 2, 64, 2 * width)
        )
        valid_part = lax.dynamic_slice(valid, (block_x, block_y, zero, zero), (1, 2, count_z, 27))[
            0
        ]
        return attend_span(query_part, region, valid_part, heads)

    result = lax.map(one_span, jnp.arange(count_x * pairs, dtype=jnp.int32))
    return result.reshape(count_x, count_y, count_z, 64, width)


def on_device(latent, norm_gain, norm_shift, w_qkv, w_out, b_out, depth_limit):
    size_x, size_y, size_z, width = latent.shape
    grouped = latent.astype(jnp.float32).reshape(-1, GROUPS, width // GROUPS)
    count = (
        grouped.shape[0]
        * grouped.shape[2]
        * lax.axis_size("gx")
        * lax.axis_size("gy")
        * lax.axis_size("gz")
    )
    mean = lax.psum(jnp.sum(grouped, axis=(0, 2)), ("gx", "gy", "gz")) / count
    centred = grouped - mean[None, :, None]
    var = lax.psum(jnp.sum(centred * centred, axis=(0, 2)), ("gx", "gy", "gz")) / count
    normed = (centred * lax.rsqrt(var + 1e-06)[None, :, None]).reshape(
        size_x, size_y, size_z, width
    )
    normed = (normed * norm_gain + norm_shift).astype(jnp.bfloat16)
    qkv = jnp.dot(normed.reshape(-1, width), w_qkv, preferred_element_type=jnp.float32).astype(
        jnp.bfloat16
    )
    queries = qkv[:, :width].reshape(size_x, size_y, size_z, width)
    keyvals = qkv[:, width:].reshape(size_x, size_y, size_z, 2 * width)
    padded = padded_2(keyvals, (("gx", 0), ("gy", 1), ("gz", 2)), 4)
    count_x, count_y, count_z = depth_limit.shape
    valid = valid_table(
        depth_limit,
        lax.axis_index("gx") * count_x,
        lax.axis_index("gy") * count_y,
        lax.axis_index("gz") * count_z,
        count_x * lax.axis_size("gx"),
        count_y * lax.axis_size("gy"),
        count_z * lax.axis_size("gz"),
    )
    mixed = from_blocks(attend_all(to_blocks(queries), to_blocks(padded), valid, HEADS))
    output = jnp.dot(mixed.reshape(-1, width), w_out, preferred_element_type=jnp.float32) + b_out
    return output.astype(jnp.bfloat16).reshape(size_x, size_y, size_z, width)


def solution(mesh):
    placed = (P("gx", "gy", "gz", None), P(), P(), P(), P(), P(), P("gx", "gy", "gz"))
    return jax.shard_map(
        on_device, mesh=mesh, in_specs=placed, out_specs=P("gx", "gy", "gz", None), check_vma=False
    )
```

profile of v0, /device:TPU:128, one launch (start us, length us, event | category | flops | bytes accessed | tf_op | source)
XLA Modules:
  0.0 813.5 jit_solution(6795876565665884142)
XLA Ops:
  1.8 76.0 %psum.14 = f32[32]{0:T(128)S(1)} all-reduce(f32[32]{0:T(128)S(1)} %reduce_sum.46), channel_id=1, replica_groups=mesh['gx'=8,'gy'=4,'gz'=8] {'gx','gy','gz'}, use_global_device_ids=true, to_apply=%region_2.0 | all-reduce | flops 32 | bytes 256 | tf_op jit(solution)/shard_map/psum | solution.py:127
  79.8 73.0 %psum.15 = f32[32]{0:T(128)S(1)} all-reduce(f32[32]{0:T(128)S(1)} %reduce_sum.49), channel_id=1, replica_groups=mesh['gx'=8,'gy'=4,'gz'=8] {'gx','gy','gz'}, use_global_device_ids=true, to_apply=%region_5.6 | all-reduce | flops 32 | bytes 256 | tf_op jit(solution)/shard_map/psum | solution.py:129
  157.7 5.8 collective-permute-start.1
  163.6 21.6 %collective-permute-done = bf16[4,16,16,512]{3,2,1,0:T(8,128)(2,1)S(1)} collective-permute-done((bf16[4,16,16,512]{3,2,1,0:T(8,128)(2,1)S(1)}, bf16[4,16,16,512]{3,2,1,0:T(8,128)(2,1)S(1)}, u32[]{:S(2)}, u32[]{:S(2)}) %collective-permute-start) | collective-permute-done | bytes 1048608 | tf_op jit(solution)/shard_map/ppermute | solution.py:24
  191.5 20.6 %collective-permute-done.2 = bf16[16,4,16,512]{3,2,1,0:T(8,128)(2,1)S(1)} collective-permute-done((bf16[16,4,16,512]{3,2,1,0:T(8,128)(2,1)S(1)}, bf16[16,4,16,512]{3,2,1,0:T(8,128)(2,1)S(1)}, u32[]{:S(2)}, u32[]{:S(2)}) %collective-permute-start.2) | collective-permute-done | bytes 1048608 | tf_op jit(solution)/shard_map/ppermute | solution.py:24
  229.7 23.6 %collective-permute-done.4 = bf16[16,24,4,512]{3,2,1,0:T(4,128)(2,1)} collective-permute-done((bf16[16,24,4,512]{3,2,1,0:T(4,128)(2,1)}, bf16[16,24,4,512]{3,2,1,0:T(4,128)(2,1)}, u32[]{:S(2)}, u32[]{:S(2)}) %collective-permute-start.4) | collective-permute-done | bytes 1572896 | tf_op jit(solution)/shard_map/ppermute | solution.py:24
  253.3 36.1 %collective-permute-done.5 = bf16[16,24,4,512]{3,2,1,0:T(4,128)(2,1)} collective-permute-done((bf16[16,24,4,512]{3,2,1,0:T(4,128)(2,1)}, bf16[16,24,4,512]{3,2,1,0:T(4,128)(2,1)}, u32[]{:S(2)}, u32[]{:S(2)}) %collective-permute-start.5) | collective-permute-done | bytes 1572896 | tf_op jit(solution)/shard_map/ppermute | solution.py:26
  289.4 10.5 %pad_maximum_fusion = bf16[16,24,24,512]{3,2,1,0:T(8,128)(2,1)} fusion(bf16[16,24,4,512]{3,2,1,0:T(4,128)(2,1)} %collective-permute-done.5, bf16[16,4,16,512]{3,2,1,0:T(8,128)(2,1)} %copy-done.4, bf16[4,16,16,512]{3,2,1,0:T(8,128)(2,1)} %copy-done.2, bf16[8,16,16,512]{3,2,1,0:T(8,128)(2,1)S(1)} %bitcast.275, ...), kind=kLoop, calls=%fused_computation.71 | loop fusion | flops 66060288 | bytes 18874368 | tf_op jit(solution)/shard_map/concatenate | solution.py:22
  299.9 14.0 %reshape.177 = bf16[4,4,6,4,6,4,512]{6,5,4,3,2,1,0:T(4,128)(2,1)} reshape(bf16[16,24,24,512]{3,2,1,0:T(8,128)(2,1)} %pad_maximum_fusion) | data formatting | bytes 18874368 | tf_op jit(solution)/shard_map/reshape | solution.py:35
  313.9 21.7 %copy.72 = bf16[4,6,6,4,4,4,512]{6,0,5,4,3,2,1:T(4,128)(2,1)} copy(bf16[4,6,6,4,4,4,512]{6,5,2,4,1,3,0:T(4,128)(2,1)} %bitcast.271) | data formatting | bytes 18874368 | tf_op jit(solution)/shard_map/transpose | solution.py:36
  335.6 9.7 %copy.74 = bf16[4,6,6,64,512]{4,3,2,1,0:T(8,128)(2,1)} copy(bf16[4,6,6,64,512]{4,0,3,2,1:T(4,128)(2,1)} %bitcast.272) | data formatting | bytes 18874368 | tf_op jit(solution)/shard_map/while | solution.py:113
  345.4 465.8 %while.12 = (s32[]{:T(128)}, bf16[4,2,4,64,256]{4,2,3,1,0:T(4,128)(2,1)S(1)}, s32[4]{0:T(128)S(1)}, bf16[4,6,6,64,512]{4,3,2,1,0:T(8,128)(2,1)}, pred[2,4,4,27]{...) while((s32[]{:T(128)}, ...), condition=%wide.region_9.10_spmd, body=%wide.region_6.9_spmd.sunk | while | flops 948569856 | bytes 158424544 | solution.py:113
  399.7 10.1 %fusion.124 = (bf16[2,4,1728,256]{3,2,1,0:T(8,128)(2,1)}, bf16[2,4,1728,256]{3,2,1,0:T(8,128)(2,1)}) fusion(bf16[2,4,1728,512]{3,2,1,0:T(8,128)(2,1)} %bitcast.268), kind=kLoop, calls=%fused_computation.105.clone.1 | loop fusion | bytes 28311552 | tf_op jit(solution)/shard_map/while/body/eval_jaxpr/slice | solution.py:78
  409.8 10.0 %copy.87 = bf16[2,4,1728,256]{2,3,1,0:T(8,128)(2,1)} copy(bf16[2,4,1728,256]{3,2,1,0:T(8,128)(2,1)} %get-tuple-element.162) | data formatting | bytes 14155776 | tf_op jit(solution)/shard_map/while/body/eval_jaxpr/slice | solution.py:78
  421.3 16.7 %fusion.126 = (f32[2,4,8,64]{3,2,1,0:T(8,128)S(1)}, f32[2,4,8,64,1728]{4,3,2,1,0:T(8,128)}) fusion(pred[2,4,1728]{2,1,0:T(4,128)(4,1)S(1)} %broadcast_in_dim.76, bf16[2,4,64,8,32]{2,4,3,1,0:T(8,128)(2,1)S(1)} %bitcast.276, bf16[2,4,1728,8,32]{2,4,3,1,0:T(8,128)(2,1)} %bitcast.269), kind=kOutput, calls=%fused_computation.106.clone.1 | convolution fusion | flops 481298112 | bytes 35681792 | tf_op jit(solution)/shard_map/while/body/eval_jaxpr/sub | solution.py:87
  438.0 10.0 %copy.85 = bf16[2,4,1728,256]{2,3,1,0:T(8,128)(2,1)} copy(bf16[2,4,1728,256]{3,2,1,0:T(8,128)(2,1)} %get-tuple-element.161) | data formatting | bytes 14155776 | tf_op jit(solution)/shard_map/while/body/eval_jaxpr/slice | solution.py:79
  448.0 13.6 %fusion.127 = bf16[2,4,8,32,64]{4,3,2,1,0:T(8,128)(2,1)S(1)} fusion(bf16[2,4,1728,8,32]{2,4,3,1,0:T(8,128)(2,1)} %bitcast.270, f32[2,4,8,64,1728]{4,3,2,1,0:T(8,128)} %get-tuple-element.163, f32[2,4,8,64]{3,2,1,0:T(8,128)S(1)} %get-tuple-element.164), kind=kOutput, calls=%fused_computation.10.clone.1 | convolution fusion | flops 467271680 | bytes 35667968 | tf_op jit(solution)/shard_map/while/body/eval_jaxpr/abhqk,abkhd->abqhd/dot_general | solution.py:89
  516.1 10.1 %fusion.124 = (bf16[2,4,1728,256]{3,2,1,0:T(8,128)(2,1)}, bf16[2,4,1728,256]{3,2,1,0:T(8,128)(2,1)}) fusion(bf16[2,4,1728,512]{3,2,1,0:T(8,128)(2,1)} %bitcast.268), kind=kLoop, calls=%fused_computation.105.clone.1 | loop fusion | bytes 28311552 | tf_op jit(solution)/shard_map/while/body/eval_jaxpr/slice | solution.py:78
  526.1 10.0 %copy.87 = bf16[2,4,1728,256]{2,3,1,0:T(8,128)(2,1)} copy(bf16[2,4,1728,256]{3,2,1,0:T(8,128)(2,1)} %get-tuple-element.162) | data formatting | bytes 14155776 | tf_op jit(solution)/shard_map/while/body/eval_jaxpr/slice | solution.py:78
  537.7 16.7 %fusion.126 = (f32[2,4,8,64]{3,2,1,0:T(8,128)S(1)}, f32[2,4,8,64,1728]{4,3,2,1,0:T(8,128)}) fusion(pred[2,4,1728]{2,1,0:T(4,128)(4,1)S(1)} %broadcast_in_dim.76, bf16[2,4,64,8,32]{2,4,3,1,0:T(8,128)(2,1)S(1)} %bitcast.276, bf16[2,4,1728,8,32]{2,4,3,1,0:T(8,128)(2,1)} %bitcast.269), kind=kOutput, calls=%fused_computation.106.clone.1 | convolution fusion | flops 481298112 | bytes 35681792 | tf_op jit(solution)/shard_map/while/body/eval_jaxpr/sub | solution.py:87
  554.4 10.0 %copy.85 = bf16[2,4,1728,256]{2,3,1,0:T(8,128)(2,1)} copy(bf16[2,4,1728,256]{3,2,1,0:T(8,128)(2,1)} %get-tuple-element.161) | data formatting | bytes 14155776 | tf_op jit(solution)/shard_map/while/body/eval_jaxpr/slice | solution.py:79
  564.4 13.6 %fusion.127 = bf16[2,4,8,32,64]{4,3,2,1,0:T(8,128)(2,1)S(1)} fusion(bf16[2,4,1728,8,32]{2,4,3,1,0:T(8,128)(2,1)} %bitcast.270, f32[2,4,8,64,1728]{4,3,2,1,0:T(8,128)} %get-tuple-element.163, f32[2,4,8,64]{3,2,1,0:T(8,128)S(1)} %get-tuple-element.164), kind=kOutput, calls=%fused_computation.10.clone.1 | convolution fusion | flops 467271680 | bytes 35667968 | tf_op jit(solution)/shard_map/while/body/eval_jaxpr/abhqk,abkhd->abqhd/dot_general | solution.py:89
  632.5 10.1 %fusion.124 = (bf16[2,4,1728,256]{3,2,1,0:T(8,128)(2,1)}, bf16[2,4,1728,256]{3,2,1,0:T(8,128)(2,1)}) fusion(bf16[2,4,1728,512]{3,2,1,0:T(8,128)(2,1)} %bitcast.268), kind=kLoop, calls=%fused_computation.105.clone.1 | loop fusion | bytes 28311552 | tf_op jit(solution)/shard_map/while/body/eval_jaxpr/slice | solution.py:78
  642.5 10.0 %copy.87 = bf16[2,4,1728,256]{2,3,1,0:T(8,128)(2,1)} copy(bf16[2,4,1728,256]{3,2,1,0:T(8,128)(2,1)} %get-tuple-element.162) | data formatting | bytes 14155776 | tf_op jit(solution)/shard_map/while/body/eval_jaxpr/slice | solution.py:78
  654.1 16.7 %fusion.126 = (f32[2,4,8,64]{3,2,1,0:T(8,128)S(1)}, f32[2,4,8,64,1728]{4,3,2,1,0:T(8,128)}) fusion(pred[2,4,1728]{2,1,0:T(4,128)(4,1)S(1)} %broadcast_in_dim.76, bf16[2,4,64,8,32]{2,4,3,1,0:T(8,128)(2,1)S(1)} %bitcast.276, bf16[2,4,1728,8,32]{2,4,3,1,0:T(8,128)(2,1)} %bitcast.269), kind=kOutput, calls=%fused_computation.106.clone.1 | convolution fusion | flops 481298112 | bytes 35681792 | tf_op jit(solution)/shard_map/while/body/eval_jaxpr/sub | solution.py:87
  670.8 10.0 %copy.85 = bf16[2,4,1728,256]{2,3,1,0:T(8,128)(2,1)} copy(bf16[2,4,1728,256]{3,2,1,0:T(8,128)(2,1)} %get-tuple-element.161) | data formatting | bytes 14155776 | tf_op jit(solution)/shard_map/while/body/eval_jaxpr/slice | solution.py:79
  680.8 13.6 %fusion.127 = bf16[2,4,8,32,64]{4,3,2,1,0:T(8,128)(2,1)S(1)} fusion(bf16[2,4,1728,8,32]{2,4,3,1,0:T(8,128)(2,1)} %bitcast.270, f32[2,4,8,64,1728]{4,3,2,1,0:T(8,128)} %get-tuple-element.163, f32[2,4,8,64]{3,2,1,0:T(8,128)S(1)} %get-tuple-element.164), kind=kOutput, calls=%fused_computation.10.clone.1 | convolution fusion | flops 467271680 | bytes 35667968 | tf_op jit(solution)/shard_map/while/body/eval_jaxpr/abhqk,abkhd->abqhd/dot_general | solution.py:89
  748.8 10.1 %fusion.124 = (bf16[2,4,1728,256]{3,2,1,0:T(8,128)(2,1)}, bf16[2,4,1728,256]{3,2,1,0:T(8,128)(2,1)}) fusion(bf16[2,4,1728,512]{3,2,1,0:T(8,128)(2,1)} %bitcast.268), kind=kLoop, calls=%fused_computation.105.clone.1 | loop fusion | bytes 28311552 | tf_op jit(solution)/shard_map/while/body/eval_jaxpr/slice | solution.py:78
  758.9 10.0 %copy.87 = bf16[2,4,1728,256]{2,3,1,0:T(8,128)(2,1)} copy(bf16[2,4,1728,256]{3,2,1,0:T(8,128)(2,1)} %get-tuple-element.162) | data formatting | bytes 14155776 | tf_op jit(solution)/shard_map/while/body/eval_jaxpr/slice | solution.py:78
  770.5 16.7 %fusion.126 = (f32[2,4,8,64]{3,2,1,0:T(8,128)S(1)}, f32[2,4,8,64,1728]{4,3,2,1,0:T(8,128)}) fusion(pred[2,4,1728]{2,1,0:T(4,128)(4,1)S(1)} %broadcast_in_dim.76, bf16[2,4,64,8,32]{2,4,3,1,0:T(8,128)(2,1)S(1)} %bitcast.276, bf16[2,4,1728,8,32]{2,4,3,1,0:T(8,128)(2,1)} %bitcast.269), kind=kOutput, calls=%fused_computation.106.clone.1 | convolution fusion | flops 481298112 | bytes 35681792 | tf_op jit(solution)/shard_map/while/body/eval_jaxpr/sub | solution.py:87
  787.2 10.0 %copy.85 = bf16[2,4,1728,256]{2,3,1,0:T(8,128)(2,1)} copy(bf16[2,4,1728,256]{3,2,1,0:T(8,128)(2,1)} %get-tuple-element.161) | data formatting | bytes 14155776 | tf_op jit(solution)/shard_map/while/body/eval_jaxpr/slice | solution.py:79
  797.2 13.6 %fusion.127 = bf16[2,4,8,32,64]{4,3,2,1,0:T(8,128)(2,1)S(1)} fusion(bf16[2,4,1728,8,32]{2,4,3,1,0:T(8,128)(2,1)} %bitcast.270, f32[2,4,8,64,1728]{4,3,2,1,0:T(8,128)} %get-tuple-element.163, f32[2,4,8,64]{3,2,1,0:T(8,128)S(1)} %get-tuple-element.164), kind=kOutput, calls=%fused_computation.10.clone.1 | convolution fusion | flops 467271680 | bytes 35667968 | tf_op jit(solution)/shard_map/while/body/eval_jaxpr/abhqk,abkhd->abqhd/dot_general | solution.py:89
  (207 shorter events, 248.4 us)
Async XLA Ops:
  0.0 154.6 %copy-start = (bf16[256,768]{1,0:T(8,128)(2,1)S(1)}, bf16[256,768]{1,0:T(8,128)(2,1)}, u32[]{:S(2)}) copy-start(bf16[256,768]{1,0:T(8,128)(2,1)} %param.13) | copy-start | bytes 1179652
  155.7 29.4 %collective-permute-start = (bf16[4,16,16,512]{3,2,1,0:T(8,128)(2,1)S(1)}, bf16[4,16,16,512]{3,2,1,0:T(8,128)(2,1)S(1)}, u32[]{:S(2)}, u32[]{:S(2)}) collective-permute-start(bf16[4,16,16,512]{3,2,1,0:T(8,128)(2,1)S(1)} %bitcast.282), channel_id=1, source_target_pairs={{0,32},{32,64},{64,96},{96,128},{128,160},{160,192},{192,224},{1,3... | collective-permute-start | bytes 3145736 | tf_op jit(solution)/shard_map/ppermute | solution.py:24
  157.7 29.3 %collective-permute-start.1 = (bf16[4,16,16,512]{3,2,1,0:T(8,128)(2,1)S(1)}, bf16[4,16,16,512]{3,2,1,0:T(8,128)(2,1)S(1)}, u32[]{:S(2)}, u32[]{:S(2)}) collective-permute-start(bf16[4,16,16,512]{3,2,1,0:T(8,128)(2,1)S(1)} %bitcast.281), channel_id=1, source_target_pairs={{32,0},{64,32},{96,64},{128,96},{160,128},{192,160},{224,192},{33,... | collective-permute-start | bytes 3145736 | tf_op jit(solution)/shard_map/ppermute | solution.py:26
  187.0 29.2 %copy-start.2 = (bf16[4,16,16,512]{3,2,1,0:T(8,128)(2,1)}, bf16[4,16,16,512]{3,2,1,0:T(8,128)(2,1)S(1)}, u32[]{:S(2)}) copy-start(bf16[4,16,16,512]{3,2,1,0:T(8,128)(2,1)S(1)} %collective-permute-done.1) | copy-start | bytes 3145732
  187.2 42.2 %copy-start.12 = (s32[27]{0:T(128)S(1)}, s32[27]{0:T(128)}, u32[]{:S(2)}) copy-start(s32[27]{0:T(128)} %constant.119) | copy-start | bytes 328
  187.2 42.2 %copy-start.11 = (s32[27]{0:T(128)S(1)}, s32[27]{0:T(128)}, u32[]{:S(2)}) copy-start(s32[27]{0:T(128)} %constant.121) | copy-start | bytes 328
  187.2 42.3 %copy-start.10 = (s32[27]{0:T(128)S(1)}, s32[27]{0:T(128)}, u32[]{:S(2)}) copy-start(s32[27]{0:T(128)} %constant.123) | copy-start | bytes 328
  187.3 42.4 %copy-start.7 = (s32[2,4,4]{2,1,0:T(4,128)S(1)}, s32[2,4,4]{2,1,0:T(4,128)}, u32[]{:S(2)}) copy-start(s32[2,4,4]{2,1,0:T(4,128)} %param.16) | copy-start | bytes 388
  187.3 42.4 %copy-start.9 = (s32[27]{0:T(128)S(1)}, s32[27]{0:T(128)}, u32[]{:S(2)}) copy-start(s32[27]{0:T(128)} %constant.124) | copy-start | bytes 328
  187.3 24.7 %collective-permute-start.2 = (bf16[16,4,16,512]{3,2,1,0:T(8,128)(2,1)S(1)}, bf16[16,4,16,512]{3,2,1,0:T(8,128)(2,1)S(1)}, u32[]{:S(2)}, u32[]{:S(2)}) collective-permute-start(bf16[16,4,16,512]{3,2,1,0:T(8,128)(2,1)S(1)} %get-tuple-element.116), channel_id=1, source_target_pairs={{0,8},{8,16},{16,24},{1,9},{9,17},{17,25},{2,10},{10,18},{18,26},{... | collective-permute-start | bytes 3145736 | tf_op jit(solution)/shard_map/ppermute | solution.py:24
  190.2 26.1 %collective-permute-start.3 = (bf16[16,4,16,512]{3,2,1,0:T(8,128)(2,1)S(1)}, bf16[16,4,16,512]{3,2,1,0:T(8,128)(2,1)S(1)}, u32[]{:S(2)}, u32[]{:S(2)}) collective-permute-start(bf16[16,4,16,512]{3,2,1,0:T(8,128)(2,1)S(1)} %get-tuple-element.117), channel_id=1, source_target_pairs={{8,0},{16,8},{24,16},{9,1},{17,9},{25,17},{10,2},{18,10},{26,18},{... | collective-permute-start | bytes 3145736 | tf_op jit(solution)/shard_map/ppermute | solution.py:26
  212.0 7.4 copy-start.3
  216.2 3.2 copy-start.4
  219.4 33.9 %collective-permute-start.4 = (bf16[16,24,4,512]{3,2,1,0:T(4,128)(2,1)}, bf16[16,24,4,512]{3,2,1,0:T(4,128)(2,1)}, u32[]{:S(2)}, u32[]{:S(2)}) collective-permute-start(bf16[16,24,4,512]{3,2,1,0:T(4,128)(2,1)} %get-tuple-element.114), channel_id=1, source_target_pairs={{0,1},{1,2},{2,3},{3,4},{4,5},{5,6},{6,7},{8,9},{9,10},{10,11},{11... | collective-permute-start | bytes 4718600 | tf_op jit(solution)/shard_map/ppermute | solution.py:24
  221.9 67.5 %collective-permute-start.5 = (bf16[16,24,4,512]{3,2,1,0:T(4,128)(2,1)}, bf16[16,24,4,512]{3,2,1,0:T(4,128)(2,1)}, u32[]{:S(2)}, u32[]{:S(2)}) collective-permute-start(bf16[16,24,4,512]{3,2,1,0:T(4,128)(2,1)} %get-tuple-element.115), channel_id=1, source_target_pairs={{1,0},{2,1},{3,2},{4,3},{5,4},{6,5},{7,6},{9,8},{10,9},{11,10},{12... | collective-permute-start | bytes 4718600 | tf_op jit(solution)/shard_map/ppermute | solution.py:26
  335.6 9.7 %copy-start.5 = (bf16[4,2,4,64,256]{4,2,3,1,0:T(4,128)(2,1)S(1)}, bf16[4,2,4,64,256]{4,2,3,1,0:T(4,128)(2,1)}, u32[]{:S(2)}) copy-start(bf16[4,2,4,64,256]{4,2,3,1,0:T(4,128)(2,1)} %custom-call.1) | copy-start | bytes 3145732
  345.4 466.7 %copy-start.6 = (bf16[256,256]{1,0:T(8,128)(2,1)S(1)}, bf16[256,256]{1,0:T(8,128)(2,1)}, u32[]{:S(2)}) copy-start(bf16[256,256]{1,0:T(8,128)(2,1)} %param.14) | copy-start | bytes 393220
  345.4 466.7 %copy-start.8 = (f32[256]{0:T(256)S(1)}, f32[256]{0:T(256)}, u32[]{:S(2)}) copy-start(f32[256]{0:T(256)} %param.15) | copy-start | bytes 3076
  811.2 2.4 copy-start.1
where the time goes:
time: 822 us; the launch traced here: 814 us
  local copies, waits for them, and re-layouts  387 us (47%)
  blocking collectives  149 us (18%)
  matrix products  124 us (15%)
  waiting for transfers between devices  108 us (13%)
  other arithmetic  19.3 us (2%)
  starting transfers between devices  15.7 us (2%)
  loops' own time  11 us (1%)
    while x104, local copies, waits for them, and re-layouts  196 us
    slice x8, local copies, waits for them, and re-layouts, attend_span(): keys = keyvals[..., :width].reshape(2, depth, 27 * 64, heads, head_dim)  80.3 us
    psum x1, blocking collectives, on_device(): mean = lax.psum(jnp.sum(grouped, axis=(0, 2)), ('gx', 'gy', 'gz')) / count  76 us
    psum x1, blocking collectives, on_device(): lax.psum(jnp.sum(centred * centred, axis=(0, 2)), ('gx', 'gy', 'gz'))  73 us
    sub x4, matrix products, attend_span(): expd = jnp.exp(scores - top)  66.7 us
    ppermute x3, waiting for transfers between devices, padded_2(): lax.ppermute(tail, axis, [(i, (i + 1) % count) for i in range(ends)])  65.7 us
    dot_general x4, matrix products, attend_span(): jnp.einsum('abhqk,abkhd->abqhd', weights, values, preferred_element_type=...  54.4 us
    ppermute x3, waiting for transfers between devices, padded_2(): lax.ppermute(head, axis, [((i + 1) % count, i) for i in range(ends)])  42.1 us
  transfers between devices with their start and end apart: 6, of which 6 were waited for; matrix products, arithmetic and copies ran while one was open for 1% of the time, Pallas kernels for 0%

commit v1 on v0

v1 whole, which is shorter than its diff:
```python
import functools

import jax
import jax.numpy as jnp
import numpy as np
from jax import lax
from jax.experimental import pallas as pl
from jax.experimental.pallas import tpu as pltpu
from jax.sharding import PartitionSpec as P

HEADS = 8
GROUPS = 32
AXES = ("gx", "gy", "gz")
f32, bf = jnp.float32, jnp.bfloat16
NT = (((1,), (1,)), ((), ()))


def attn_kernel(
    scal, x_ref, mean_ref, mul_ref, shift_ref, wqT, wk, wvT, wo, bo, out_ref, n_ref, k_ref, vt_ref, qbd_ref, s_ref
):
    mean, mul, shift = mean_ref[...], mul_ref[...], shift_ref[...]

    def prep_col(c, carry):
        y, z = c // 6, c % 6
        ys, zs = scal[52 + y], scal[58 + z]
        xs = jnp.concatenate([x_ref[scal[48 + i], ys, zs] for i in range(4)], axis=0)
        n = ((xs.astype(f32) - mean) * mul + shift).astype(bf)
        n_ref[c] = n
        k_ref[c] = jnp.dot(n, wk[...], preferred_element_type=f32).astype(bf)
        vt = lax.dot_general(wvT[...], n, NT, preferred_element_type=f32)
        lane = lax.broadcasted_iota(jnp.int32, (1, 256), 1) // 64
        yz = scal[36 + y] * scal[42 + z]
        val = jnp.zeros((1, 256), f32)
        for i in range(4):
            val = jnp.where(lane == i, (scal[32 + i] * yz).astype(f32), val)
        vt = vt * val
        row = lax.broadcasted_iota(jnp.int32, (16, 256), 0)
        ones = jnp.where(row == 0, jnp.broadcast_to(val, (16, 256)), 0.0)
        for g in range(2):
            t = jnp.concatenate([vt[g * 128 : (g + 1) * 128], ones], axis=0)
            vt_ref[0, c, g] = t[:, :192].astype(bf)
            vt_ref[1, c, g] = pltpu.roll(t, 192, 1)[:, :192].astype(bf)
        return carry

    lax.fori_loop(0, 36, prep_col, 0)

    rr = lax.broadcasted_iota(jnp.int32, (128, 256), 0) // 32
    ll = lax.broadcasted_iota(jnp.int32, (128, 256), 1) // 64
    diag = rr == ll
    ri = lax.broadcasted_iota(jnp.int32, (64, 256), 0)
    li = lax.broadcasted_iota(jnp.int32, (64, 256), 1) % 64
    rT = jnp.where(ri == li, 1.0, 0.0).astype(bf)
    scale = float(np.log2(np.e) / np.sqrt(32.0))

    def query(i, carry):
        bx, by, bz = i // 16, (i // 4) % 4, i % 4
        c0 = (by + 1) * 6 + bz + 1
        nq = n_ref[c0, pl.ds(pl.multiple_of((bx + 1) * 64, 64), 64), :]
        n4 = jnp.concatenate([nq] * 4, axis=0)
        qt = lax.dot_general(wqT[...], n4, NT, preferred_element_type=f32)
        qt = (qt * scale).astype(bf)
        for g in range(2):
            qbd_ref[g] = jnp.where(diag, qt[g * 128 : (g + 1) * 128], jnp.zeros((), bf))
        r0 = pl.multiple_of(bx * 64, 64)

        def body(cols):
            tops = []
            for g in range(2):
                m = None
                for j, (dy, dz) in enumerate(cols):
                    c = (by + dy) * 6 + bz + dz
                    kt = k_ref[c, pl.ds(r0, 192), g * 128 : (g + 1) * 128]
                    s = jnp.dot(kt, qbd_ref[g], preferred_element_type=f32)
                    s_ref[g, j] = s
                    mm = jnp.max(s.reshape(24, 8, 256), axis=0)
                    m = mm if m is None else jnp.maximum(m, mm)
                tops.append(jnp.max(m, axis=0, keepdims=True))
            mixed = []
            for g in range(2):
                o = jnp.zeros((144, 256), f32)
                for j, (dy, dz) in enumerate(cols):
                    c = (by + dy) * 6 + bz + dz
                    p = jnp.exp2(s_ref[g, j] - tops[g]).astype(bf)
                    o = o + jnp.dot(vt_ref[bx, c, g], p, preferred_element_type=f32)
                om = o[:128] * (1.0 / o[128:129])
                om = jnp.where(diag, om, 0.0).astype(bf)
                mixed.append(lax.dot_general(rT, om, NT, preferred_element_type=f32).astype(bf))
            out = jnp.dot(jnp.concatenate(mixed, axis=1), wo[...], preferred_element_type=f32) + bo[...]
            out_ref[bx, by, bz] = out.astype(bf)

        limit = scal[i]

        @pl.when(limit == 0)
        def _near():
            body([(dy, 1) for dy in range(3)])

        @pl.when(limit != 0)
        def _full():
            body([(dy, dz) for dz in range(3) for dy in range(3)])

        return carry

    lax.fori_loop(0, 32, query, 0)


def attend(*args):
    vmem = pl.BlockSpec(memory_space=pltpu.VMEM)
    return pl.pallas_call(
        attn_kernel,
        out_shape=jax.ShapeDtypeStruct((2, 4, 4, 64, 256), bf),
        in_specs=[pl.BlockSpec(memory_space=pltpu.SMEM)] + [vmem] * 9,
        out_specs=vmem,
        scratch_shapes=[
            pltpu.VMEM((36, 256, 256), bf),
            pltpu.VMEM((36, 256, 256), bf),
            pltpu.VMEM((2, 36, 2, 144, 192), bf),
            pltpu.VMEM((2, 128, 256), bf),
            pltpu.VMEM((2, 9, 192, 256), f32),
        ],
        compiler_params=pltpu.CompilerParams(vmem_limit_bytes=56 * 2**20),
    )(*args)


def to_blocks(field):
    size_x, size_y, size_z, chans = field.shape
    shaped = field.reshape(size_x // 4, 4, size_y // 4, 4, size_z // 4, 4, chans)
    return shaped.transpose(0, 2, 4, 1, 3, 5, 6).reshape(size_x // 4, size_y // 4, size_z // 4, 64, chans)


def from_blocks(blocks):
    count_x, count_y, count_z, cells, chans = blocks.shape
    shaped = blocks.reshape(count_x, count_y, count_z, 4, 4, 4, chans)
    return shaped.transpose(0, 3, 1, 4, 2, 5, 6).reshape(count_x * 4, count_y * 4, count_z * 4, chans)


def padded(blocks, axis, dim):
    count = lax.axis_size(axis)
    head = lax.slice_in_dim(blocks, 0, 1, axis=dim)
    tail = lax.slice_in_dim(blocks, blocks.shape[dim] - 1, blocks.shape[dim], axis=dim)
    up = [(i, i + 1) for i in range(count - 1)]
    down = [(i + 1, i) for i in range(count - 1)]
    return jnp.concatenate(
        [lax.ppermute(tail, axis, up), blocks, lax.ppermute(head, axis, down)], axis=dim
    )


def group_stats(latent):
    width = latent.shape[-1]
    cells = latent.astype(f32).reshape(-1, width)
    per = width // GROUPS
    entries = cells.shape[0] * per
    means = jnp.sum(jnp.sum(cells, axis=0).reshape(GROUPS, per), axis=1) / entries
    centred = cells - jnp.repeat(means, per)[None, :]
    squares = jnp.sum(jnp.sum(centred * centred, axis=0).reshape(GROUPS, per), axis=1)
    count = lax.axis_size(AXES)
    mine = jnp.concatenate([means, squares, jnp.zeros((64,), f32)])
    every = lax.all_to_all(jnp.broadcast_to(mine[None], (count, 128)), AXES, 0, 0, tiled=True)
    mean = jnp.sum(every[:, :32], axis=0) / count
    apart = every[:, :32] - mean[None]
    var = (jnp.sum(every[:, 32:64], axis=0) / entries + jnp.sum(apart * apart, axis=0)) / count
    return mean, var


def scalars(depth_limit):
    parts, sources = [depth_limit.reshape(-1)], []
    for axis, inner in zip(AXES, depth_limit.shape):
        spots = np.arange(inner + 2)
        index, ends = lax.axis_index(axis), lax.axis_size(axis) - 1
        outside = ((spots == 0) & (index == 0)) | ((spots == inner + 1) & (index == ends))
        parts.append(1 - outside.astype(jnp.int32))
        sources.append(jnp.where(outside, np.clip(spots, 1, inner), spots).astype(jnp.int32))
    return jnp.concatenate(parts + sources)


def on_device(latent, norm_gain, norm_shift, w_qkv, w_out, b_out, depth_limit):
    width = latent.shape[-1]
    blocks = to_blocks(latent)
    for axis, dim in (("gz", 2), ("gx", 0), ("gy", 1)):
        blocks = padded(blocks, axis, dim)
    mean, var = group_stats(latent)
    per = width // GROUPS
    mul = jnp.repeat(lax.rsqrt(var + 1e-06), per) * norm_gain
    mean = jnp.repeat(mean, per)
    out = attend(
        scalars(depth_limit),
        blocks,
        mean[None],
        mul[None],
        norm_shift[None],
        w_qkv[:, :width].T,
        w_qkv[:, width : 2 * width],
        w_qkv[:, 2 * width :].T,
        w_out,
        b_out[None],
    )
    return from_blocks(out)


def solution(mesh):
    placed = (P("gx", "gy", "gz", None), P(), P(), P(), P(), P(), P("gx", "gy", "gz"))
    return jax.shard_map(
        on_device, mesh=mesh, in_specs=placed, out_specs=P("gx", "gy", "gz", None), check_vma=False
    )
```

time: 822 us -> 159 us (0.19)
  local copies, waits for them, and re-layouts: 387 us -> 16.7 us
  blocking collectives: 149 us -> 0 us
  matrix products: 124 us -> 0 us
  waiting for transfers between devices: 108 us -> 28.7 us
  Pallas kernels: 0 us -> 72.3 us
  starting transfers between devices: 15.7 us -> 30.2 us
  loops' own time: 11 us -> 0 us
  other arithmetic: 19.3 us -> 9.55 us
    while x105 -> x0, local copies, waits for them, and re-layouts: 206 us -> none
    psum x2 -> x0, blocking collectives: 149 us -> none  [the longest x1 76 us: on_device(): mean = lax.psum(jnp.sum(grouped, axis=(0, 2)), ('gx', 'gy', 'gz')) / count]
    slice x15 -> x3, local copies, waits for them, and re-layouts: 122 us -> 3.08 us  [the longest x1 1.71 us: on_device(): w_qkv[:, 2 * width:]]
    ppermute x6, waiting for transfers between devices: 108 us -> 28.7 us  [the longest x3 15.7 us: padded(): lax.ppermute(tail, axis, up)]
    pallas_call x0 -> x1, Pallas kernels: none -> 72.3 us  [attend(): pl.pallas_call(attn_kernel, out_shape=jax.ShapeDtypeStruct((2, 4, 4, 64,...]
    sub x4 -> x0, matrix products: 66.7 us -> none  [attend_span(): expd = jnp.exp(scores - top)]
    dot_general x6 -> x0, matrix products: 56.8 us -> none  [the longest x4 54.4 us: attend_span(): jnp.einsum('abhqk,abkhd->abqhd', weights, values, preferred_element_type=...]
    transpose x1 -> x0, local copies, waits for them, and re-layouts: 21.7 us -> none  [to_blocks(): shaped.transpose(0, 2, 4, 1, 3, 5, 6)]
  transfers between devices with their start and end apart: 6 -> 7, of which waited for: 6 -> 6; matrix products, arithmetic and copies ran while one was open for 1% -> 9% of each run, Pallas kernels for 0% -> 0%
where the time goes in v1:
time: 159 us; the launch traced here: 158 us
  Pallas kernels  72.3 us (45%)
  starting transfers between devices  30.2 us (19%)
  waiting for transfers between devices  28.7 us (18%)
  local copies, waits for them, and re-layouts  16.7 us (11%)
  other arithmetic  9.55 us (6%)
    pallas_call x1, Pallas kernels, attend(): pl.pallas_call(attn_kernel, out_shape=jax.ShapeDtypeStruct((2, 4, 4, 64,...  72.3 us
    ppermute x3, waiting for transfers between devices, padded(): lax.ppermute(tail, axis, up)  15.7 us
    all_to_all x1, starting transfers between devices, group_stats(): lax.all_to_all(jnp.broadcast_to(mine[None], (count, 128)), AXES, 0, 0, ti...  13.5 us
    ppermute x3, waiting for transfers between devices, padded(): lax.ppermute(head, axis, down)  13 us
    ppermute x3, starting transfers between devices, padded(): lax.ppermute(tail, axis, up)  8.36 us
    ppermute x3, starting transfers between devices, padded(): lax.ppermute(head, axis, down)  8.34 us
    concatenate x1, other arithmetic, padded(): jnp.concatenate([lax.ppermute(tail, axis, up), blocks, lax.ppermute(head,...  4.09 us
  transfers between devices with their start and end apart: 7, of which 6 were waited for; matrix products, arithmetic and copies ran while one was open for 9% of the time, Pallas kernels for 0%

profile of v1, /device:TPU:128, one launch (start us, length us, event | category | flops | bytes accessed | tf_op | source)
XLA Modules:
  0.0 157.8 jit_solution(13972471584928184450)
XLA Ops:
  0.0 1.3 reshape.41
  1.3 1.6 copy.47
  2.9 1.4 reshape.42
  4.4 2.9 %collective-permute-start = (bf16[2,4,1,64,256]{4,3,2,1,0:T(8,128)(2,1)S(1)}, bf16[2,4,1,64,256]{4,3,2,1,0:T(8,128)(2,1)S(1)}, u32[]{:S(2)}, u32[]{:S(2)}) collective-permute-start(bf16[2,4,1,64,256]{4,3,2,1,0:T(8,128)(2,1)S(1)} %get-tuple-element.12), channel_id=1, source_target_pairs={{0,1},{1,2},{2,3},{3,4},{4,5},{5,6},{6,7},{8,9},{9,10},{10,11},{11... | collective-permute-start | bytes 786440 | tf_op jit(solution)/shard_map/ppermute | solution.py:143
  7.4 1.3 collective-permute-start.1
  9.2 3.7 %collective-permute-done = bf16[2,4,1,64,256]{4,3,2,1,0:T(8,128)(2,1)S(1)} collective-permute-done((bf16[2,4,1,64,256]{4,3,2,1,0:T(8,128)(2,1)S(1)}, bf16[2,4,1,64,256]{4,3,2,1,0:T(8,128)(2,1)S(1)}, u32[]{:S(2)}, u32[]{:S(2)}) %collective-permute-start) | collective-permute-done | bytes 262176 | tf_op jit(solution)/shard_map/ppermute | solution.py:143
  12.9 1.3 constant_dynamic-update-slice_fusion.1
  14.2 6.7 %collective-permute-done.1 = bf16[2,4,1,64,256]{4,3,2,1,0:T(8,128)(2,1)S(1)} collective-permute-done((bf16[2,4,1,64,256]{4,3,2,1,0:T(8,128)(2,1)S(1)}, bf16[2,4,1,64,256]{4,3,2,1,0:T(8,128)(2,1)S(1)}, u32[]{:S(2)}, u32[]{:S(2)}) %collective-permute-start.1) | collective-permute-done | bytes 262176 | tf_op jit(solution)/shard_map/ppermute | solution.py:143
  21.0 1.3 fusion.2
  22.3 1.9 %collective-permute-start.2 = (bf16[1,4,6,64,256]{4,3,2,1,0:T(8,128)(2,1)}, bf16[1,4,6,64,256]{4,3,2,1,0:T(8,128)(2,1)S(1)}, u32[]{:S(2)}, u32[]{:S(2)}) collective-permute-start(bf16[1,4,6,64,256]{4,3,2,1,0:T(8,128)(2,1)} %get-tuple-element.9), channel_id=1, source_target_pairs={{0,32},{32,64},{64,96},{96,128},{128,160},{160,192},{192,224},{1,3... | collective-permute-start | bytes 2359304 | tf_op jit(solution)/shard_map/ppermute | solution.py:143
  24.2 5.8 %collective-permute-start.3 = (bf16[1,4,6,64,256]{4,3,2,1,0:T(8,128)(2,1)}, bf16[1,4,6,64,256]{4,3,2,1,0:T(8,128)(2,1)}, u32[]{:S(2)}, u32[]{:S(2)}) collective-permute-start(bf16[1,4,6,64,256]{4,3,2,1,0:T(8,128)(2,1)} %get-tuple-element.10), channel_id=1, source_target_pairs={{32,0},{64,32},{96,64},{128,96},{160,128},{192,160},{224,192},{33,... | collective-permute-start | bytes 2359304 | tf_op jit(solution)/shard_map/ppermute | solution.py:143
  30.8 0.7 broadcast_in_dim.30
  31.5 13.5 %all-to-all-start = ((f32[256,1,128]{2,1,0:T(1,128)}), f32[256,1,128]{2,1,0:T(1,128)S(1)}, u32[]{:S(2)}, u32[]{:S(2)}) async-start(f32[256,1,128]{2,1,0:T(1,128)} %broadcast_in_dim.30), calls=%async_computation | async-start | bytes 262144 | tf_op jit(solution)/shard_map/all_to_all | solution.py:157
  45.1 0.6 iota_select_fusion
  45.7 1.7 %fusion.4 = (bf16[256,256]{1,0:T(8,128)(2,1)S(1)}, bf16[256,256]{1,0:T(8,128)(2,1)S(1)}, bf16[256,256]{1,0:T(8,128)(2,1)}) fusion(bf16[256,768]{1,0:T(8,128)(2,1)} %param.22), kind=kLoop, calls=%fused_computation.30 | loop fusion | bytes 786432 | tf_op jit(solution)/shard_map/slice | solution.py:192
  47.4 1.0 collective-permute-done.2
  48.4 1.6 %collective-permute-done.3 = bf16[1,4,6,64,256]{4,3,2,1,0:T(8,128)(2,1)} collective-permute-done((bf16[1,4,6,64,256]{4,3,2,1,0:T(8,128)(2,1)}, bf16[1,4,6,64,256]{4,3,2,1,0:T(8,128)(2,1)}, u32[]{:S(2)}, u32[]{:S(2)}) %collective-permute-start.3) | collective-permute-done | bytes 786464 | tf_op jit(solution)/shard_map/ppermute | solution.py:143
  50.0 2.3 %pad_maximum_fusion.3 = (bf16[4,1,6,64,256]{4,3,2,1,0:T(8,128)(2,1)}, bf16[4,1,6,64,256]{4,3,2,1,0:T(8,128)(2,1)}) fusion(bf16[1,4,6,64,256]{4,3,2,1,0:T(8,128)(2,1)} %collective-permute-done.3, bf16[2,4,6,64,256]{4,3,2,1,0:T(8,128)(2,1)S(1)} %constant_dynamic-update-slice_fusion, bf16[1,4,6,64,256]{4,3,2,1,0:T(8,128)(2,1)S(1)} %collective-permute-done.2), kind=kLoop, calls=%fused_computation.8 | loop fusion | flops 1572864 | bytes 4718592 | tf_op jit(solution)/shard_map/slice | solution.py:139
  52.3 3.5 %collective-permute-start.4 = (bf16[4,1,6,64,256]{4,3,2,1,0:T(8,128)(2,1)}, bf16[4,1,6,64,256]{4,3,2,1,0:T(8,128)(2,1)S(1)}, u32[]{:S(2)}, u32[]{:S(2)}) collective-permute-start(bf16[4,1,6,64,256]{4,3,2,1,0:T(8,128)(2,1)} %get-tuple-element.7), channel_id=1, source_target_pairs={{0,8},{8,16},{16,24},{1,9},{9,17},{17,25},{2,10},{10,18},{18,26},{... | collective-permute-start | bytes 2359304 | tf_op jit(solution)/shard_map/ppermute | solution.py:143
  55.8 1.3 collective-permute-start.5
  57.3 0.8 copy.44
  58.0 0.8 copy.45
  58.8 1.3 concatenate.15.scal
  60.8 0.7 broadcast_in_dim_reshape.4.mean_ref
  61.4 1.3 mul.12
  62.7 11.0 %collective-permute-done.4 = bf16[4,1,6,64,256]{4,3,2,1,0:T(8,128)(2,1)S(1)} collective-permute-done((bf16[4,1,6,64,256]{4,3,2,1,0:T(8,128)(2,1)}, bf16[4,1,6,64,256]{4,3,2,1,0:T(8,128)(2,1)S(1)}, u32[]{:S(2)}, u32[]{:S(2)}) %collective-permute-start.4) | collective-permute-done | bytes 786464 | tf_op jit(solution)/shard_map/ppermute | solution.py:143
  73.7 4.7 %collective-permute-done.5 = bf16[4,1,6,64,256]{4,3,2,1,0:T(8,128)(2,1)} collective-permute-done((bf16[4,1,6,64,256]{4,3,2,1,0:T(8,128)(2,1)}, bf16[4,1,6,64,256]{4,3,2,1,0:T(8,128)(2,1)}, u32[]{:S(2)}, u32[]{:S(2)}) %collective-permute-start.5) | collective-permute-done | bytes 786464 | tf_op jit(solution)/shard_map/ppermute | solution.py:143
  78.4 4.1 %pad_maximum_fusion.x_ref = bf16[4,6,6,64,256]{4,3,2,1,0:T(8,128)(2,1)} fusion(bf16[4,1,6,64,256]{4,3,2,1,0:T(8,128)(2,1)} %collective-permute-done.5, bf16[1,4,6,64,256]{4,3,2,1,0:T(8,128)(2,1)} %collective-permute-done.3, bf16[2,4,6,64,256]{4,3,2,1,0:T(8,128)(2,1)S(1)} %constant_dynamic-update-slice_fusion, ...), kind=kLoop, calls=%fused_computation | loop fusion | flops 9437184 | bytes 9437184 | tf_op jit(solution)/shard_map/concatenate | solution.py:142
  82.5 72.3 %shard_map.181 = bf16[2,4,4,64,256]{4,3,2,1,0:T(8,128)(2,1)} custom-call(s32[64]{0:T(128)} %concatenate.15.scal, bf16[4,6,6,64,256]{4,3,2,1,0:T(8,128)(2,1)} %pad_maximum_fusion.x_ref, f32[1,256]{1,0:T(1,128)} %broadcast_in_dim_reshape.4.mean_ref, f32[1,256]{1,0:T(1,128)} %bitcast.20, f32[1,256]{1,0:T(1,128)} %bitcast.21, bf16[256,256]{1,0:T(8,128)(2,1)} %bitcast.16, ...), custom_call_target="tpu_custom_call" | custom-call | tf_op jit(solution)/shard_map/pallas_call | solution.py:108
  154.8 1.3 reshape.46
  156.2 0.5 copy.43
  156.7 1.1 reshape.47
  (43 shorter events, 2.1 us)
Async XLA Ops:
  2.9 5.7 %copy-start = (bf16[8,16,16,256]{3,2,1,0:T(8,128)(2,1)S(1)}, bf16[8,16,16,256]{3,2,1,0:T(8,128)(2,1)}, u32[]{:S(2)}) copy-start(bf16[8,16,16,256]{3,2,1,0:T(8,128)(2,1)} %param.19) | copy-start | bytes 3145732
  4.3 4.8 %copy-start.1 = (bf16[2,4,4,64,256]{4,3,2,1,0:T(8,128)(2,1)}, bf16[2,4,4,64,256]{4,3,2,1,0:T(8,128)(2,1)S(1)}, u32[]{:S(2)}) copy-start(bf16[2,4,4,64,256]{4,3,2,1,0:T(8,128)(2,1)S(1)} %reshape.42) | copy-start | bytes 3145732
  4.4 8.5 %collective-permute-start = (bf16[2,4,1,64,256]{4,3,2,1,0:T(8,128)(2,1)S(1)}, bf16[2,4,1,64,256]{4,3,2,1,0:T(8,128)(2,1)S(1)}, u32[]{:S(2)}, u32[]{:S(2)}) collective-permute-start(bf16[2,4,1,64,256]{4,3,2,1,0:T(8,128)(2,1)S(1)} %get-tuple-element.12), channel_id=1, source_target_pairs={{0,1},{1,2},{2,3},{3,4},{4,5},{5,6},{6,7},{8,9},{9,10},{10,11},{11... | collective-permute-start | bytes 786440 | tf_op jit(solution)/shard_map/ppermute | solution.py:143
  7.4 13.5 %collective-permute-start.1 = (bf16[2,4,1,64,256]{4,3,2,1,0:T(8,128)(2,1)S(1)}, bf16[2,4,1,64,256]{4,3,2,1,0:T(8,128)(2,1)S(1)}, u32[]{:S(2)}, u32[]{:S(2)}) collective-permute-start(bf16[2,4,1,64,256]{4,3,2,1,0:T(8,128)(2,1)S(1)} %get-tuple-element.11), channel_id=1, source_target_pairs={{1,0},{2,1},{3,2},{4,3},{5,4},{6,5},{7,6},{9,8},{10,9},{11,10},{12... | collective-permute-start | bytes 786440 | tf_op jit(solution)/shard_map/ppermute | solution.py:143
  20.9 24.1 %copy-start.6 = (pred[6]{0:T(512)(128)(4,1)S(1)}, pred[6]{0:T(512)(128)(4,1)}, u32[]{:S(2)}) copy-start(pred[6]{0:T(512)(128)(4,1)} %constant.53.clone) | copy-start | bytes 22
  20.9 24.1 %copy-start.7 = (pred[6]{0:T(512)(128)(4,1)S(1)}, pred[6]{0:T(512)(128)(4,1)}, u32[]{:S(2)}) copy-start(pred[6]{0:T(512)(128)(4,1)} %constant.54.clone) | copy-start | bytes 22
  20.9 24.1 %copy-start.8 = (s32[6]{0:T(128)S(1)}, s32[6]{0:T(128)}, u32[]{:S(2)}) copy-start(s32[6]{0:T(128)} %constant.55.clone) | copy-start | bytes 76
  22.3 26.1 %collective-permute-start.2 = (bf16[1,4,6,64,256]{4,3,2,1,0:T(8,128)(2,1)}, bf16[1,4,6,64,256]{4,3,2,1,0:T(8,128)(2,1)S(1)}, u32[]{:S(2)}, u32[]{:S(2)}) collective-permute-start(bf16[1,4,6,64,256]{4,3,2,1,0:T(8,128)(2,1)} %get-tuple-element.9), channel_id=1, source_target_pairs={{0,32},{32,64},{64,96},{96,128},{128,160},{160,192},{192,224},{1,3... | collective-permute-start | bytes 2359304 | tf_op jit(solution)/shard_map/ppermute | solution.py:143
  24.2 25.8 %collective-permute-start.3 = (bf16[1,4,6,64,256]{4,3,2,1,0:T(8,128)(2,1)}, bf16[1,4,6,64,256]{4,3,2,1,0:T(8,128)(2,1)}, u32[]{:S(2)}, u32[]{:S(2)}) collective-permute-start(bf16[1,4,6,64,256]{4,3,2,1,0:T(8,128)(2,1)} %get-tuple-element.10), channel_id=1, source_target_pairs={{32,0},{64,32},{96,64},{128,96},{160,128},{192,160},{224,192},{33,... | collective-permute-start | bytes 2359304 | tf_op jit(solution)/shard_map/ppermute | solution.py:143
  31.5 28.6 %all-to-all-start = ((f32[256,1,128]{2,1,0:T(1,128)}), f32[256,1,128]{2,1,0:T(1,128)S(1)}, u32[]{:S(2)}, u32[]{:S(2)}) async-start(f32[256,1,128]{2,1,0:T(1,128)} %broadcast_in_dim.30), calls=%async_computation | async-start | bytes 262144 | tf_op jit(solution)/shard_map/all_to_all | solution.py:157
  47.4 9.8 %copy-start.3 = (pred[4]{0:T(512)(128)(4,1)S(1)}, pred[4]{0:T(512)(128)(4,1)}, u32[]{:S(2)}) copy-start(pred[4]{0:T(512)(128)(4,1)} %constant.50.clone) | copy-start | bytes 16
  47.4 9.8 %copy-start.4 = (pred[4]{0:T(512)(128)(4,1)S(1)}, pred[4]{0:T(512)(128)(4,1)}, u32[]{:S(2)}) copy-start(pred[4]{0:T(512)(128)(4,1)} %constant.51.clone) | copy-start | bytes 16
  47.4 9.8 %copy-start.5 = (s32[4]{0:T(128)S(1)}, s32[4]{0:T(128)}, u32[]{:S(2)}) copy-start(s32[4]{0:T(128)} %constant.52.clone) | copy-start | bytes 52
  47.4 9.8 %copy-start.2 = (s32[2,4,4]{2,1,0:T(4,128)S(1)}, s32[2,4,4]{2,1,0:T(4,128)}, u32[]{:S(2)}) copy-start(s32[2,4,4]{2,1,0:T(4,128)} %param.25) | copy-start | bytes 388
  52.3 21.4 %collective-permute-start.4 = (bf16[4,1,6,64,256]{4,3,2,1,0:T(8,128)(2,1)}, bf16[4,1,6,64,256]{4,3,2,1,0:T(8,128)(2,1)S(1)}, u32[]{:S(2)}, u32[]{:S(2)}) collective-permute-start(bf16[4,1,6,64,256]{4,3,2,1,0:T(8,128)(2,1)} %get-tuple-element.7), channel_id=1, source_target_pairs={{0,8},{8,16},{16,24},{1,9},{9,17},{17,25},{2,10},{10,18},{18,26},{... | collective-permute-start | bytes 2359304 | tf_op jit(solution)/shard_map/ppermute | solution.py:143
  55.8 22.6 %collective-permute-start.5 = (bf16[4,1,6,64,256]{4,3,2,1,0:T(8,128)(2,1)}, bf16[4,1,6,64,256]{4,3,2,1,0:T(8,128)(2,1)}, u32[]{:S(2)}, u32[]{:S(2)}) collective-permute-start(bf16[4,1,6,64,256]{4,3,2,1,0:T(8,128)(2,1)} %get-tuple-element.8), channel_id=1, source_target_pairs={{8,0},{16,8},{24,16},{9,1},{17,9},{25,17},{10,2},{18,10},{26,18},{... | collective-permute-start | bytes 2359304 | tf_op jit(solution)/shard_map/ppermute | solution.py:143
